TPU v7x, 32 devices: a whole 2x2x4 slice. The times are simulated.
32 devices in a mesh: row: 8 (over z, x), col: 4 (over y, core).
Axes of the slice: x: 2, y: 2, z: 4, core: 2. Of those that a mesh axis runs over, the one named last changes fastest.
Arguments:
- tiles: bfloat16 [8, 4, 64, 128, 128], P('row', 'col'), may hold values from -0.078125 to 0.078125
- positions: int32 [8, 4, 64], replicated, may hold values from 0 to 15, as said below
- demand: bfloat16 [16384, 128], P(('row', 'col')), may hold values from -6 to 6
- value_added: bfloat16 [16384, 128], P(('row', 'col')), may hold values from -6 to 6
- extracted: int32 [128], replicated, may hold values from 0 to 127
Outputs:
- quantity: float32 [16384, 128], P(('row', 'col'))
- price: float32 [16384, 128], P(('row', 'col'))
Inputs may be any that keep to these rules, and one draw needn't show every extreme that they name: Within each device's slots d * 2 to d * 2 + 1 the 2 positions differ.
All inputs are finite; a program needn't handle non-finite values.
Results may differ from a plain program's by a relative error of at most 0.0011.
Values may be sent and summed in bfloat16 or wider, within the bound.
A program may use at most 192 MiB of HBM per device.

v0:
```python
import jax
import jax.numpy as jnp
from jax import lax
from jax.sharding import PartitionSpec as P

TERMS = 3
GROUPS = 128


def supply_term(vector, own_tiles, local_rows, local_columns, block_rows, tile_size):
    scenarios = vector.shape[1]
    gathered = lax.all_gather(vector, "row", axis=0, tiled=True)
    picked = gathered.reshape(-1, tile_size, scenarios)[local_columns]
    products = jnp.einsum("ntk,nks->nts", own_tiles, picked, preferred_element_type=jnp.float32)
    selector = (jnp.arange(block_rows, dtype=jnp.int32)[:, None] == local_rows[None, :]).astype(
        jnp.float32
    )
    partial_value = jnp.einsum("rn,nts->rts", selector, products, precision=lax.Precision.HIGHEST)
    return lax.psum_scatter(
        partial_value.reshape(-1, scenarios), "col", scatter_dimension=0, tiled=True
    )


def charge_term(vector, moved_tiles, local_rows, local_columns, block_rows, tile_size):
    scenarios = vector.shape[1]
    gathered = lax.all_gather(vector, "row", axis=0, tiled=True)
    picked = gathered.reshape(-1, tile_size, scenarios)[local_columns]
    products = jnp.einsum("nkt,nks->nts", moved_tiles, picked, preferred_element_type=jnp.float32)
    selector = (jnp.arange(block_rows, dtype=jnp.int32)[:, None] == local_rows[None, :]).astype(
        jnp.float32
    )
    partial_value = jnp.einsum("rn,nts->rts", selector, products, precision=lax.Precision.HIGHEST)
    return lax.psum_scatter(
        partial_value.reshape(-1, scenarios), "col", scatter_dimension=0, tiled=True
    )


def shards(tiles, positions, demand, value_added, extracted):
    row_devices = lax.axis_size("row")
    column_devices = lax.axis_size("col")
    row_index = lax.axis_index("row")
    column_index = lax.axis_index("col")
    tile_size = tiles.shape[-1]
    slot_count = tiles.shape[2]
    own_tiles = tiles.reshape(slot_count, tile_size, tile_size)
    scenarios = demand.shape[1]
    quarter = demand.shape[0] // tile_size
    block_rows = quarter * column_devices
    capacity = slot_count // (row_devices * column_devices)
    slot_index = jnp.arange(slot_count, dtype=jnp.int32)
    target = slot_index // capacity
    own_places = lax.dynamic_slice(
        positions, (row_index, column_index, 0), (1, 1, slot_count)
    ).reshape(slot_count)
    local_rows = target % column_devices * quarter + own_places // quarter
    local_columns = target // column_devices * quarter + own_places % quarter
    first_block = row_index * block_rows + column_index * quarter
    blocks = first_block + jnp.arange(quarter, dtype=jnp.int32)
    keep_mask = (blocks[:, None] % GROUPS != extracted[None, :]).astype(jnp.float32)[:, None, :]
    quantity = (
        keep_mask * demand.reshape(quarter, tile_size, scenarios).astype(jnp.float32)
    ).reshape(-1, scenarios)
    move = quantity.astype(jnp.bfloat16)
    for term_number in range(TERMS):
        image = supply_term(move, own_tiles, local_rows, local_columns, block_rows, tile_size)
        masked = (keep_mask * image.reshape(quarter, tile_size, scenarios)).reshape(-1, scenarios)
        quantity = quantity + masked
        if term_number + 1 < TERMS:
            move = masked.astype(jnp.bfloat16)
    price = (
        keep_mask * value_added.reshape(quarter, tile_size, scenarios).astype(jnp.float32)
    ).reshape(-1, scenarios)
    charge = price.astype(jnp.bfloat16)
    moved_tiles = lax.all_to_all(own_tiles, ("row", "col"), split_axis=0, concat_axis=0, tiled=True)
    self_index = row_index * column_devices + column_index
    table = positions.reshape(row_devices * column_devices, slot_count)
    arrived = lax.dynamic_slice_in_dim(table, self_index * capacity, capacity, axis=1).reshape(
        slot_count
    )
    source_row = target // column_devices
    source_column = target % column_devices
    moved_rows = source_column * quarter + arrived % quarter
    moved_columns = source_row * quarter + arrived // quarter
    for term_number in range(TERMS):
        cost_image = charge_term(
            charge, moved_tiles, moved_rows, moved_columns, block_rows, tile_size
        )
        masked = (keep_mask * cost_image.reshape(quarter, tile_size, scenarios)).reshape(
            -1, scenarios
        )
        price = price + masked
        if term_number + 1 < TERMS:
            charge = masked.astype(jnp.bfloat16)
    return (quantity, price)


def solution(mesh):
    placed = (
        P("row", "col", None, None, None),
        P(),
        P(("row", "col"), None),
        P(("row", "col"), None),
        P(),
    )
    return jax.shard_map(
        shards,
        mesh=mesh,
        in_specs=placed,
        out_specs=(P(("row", "col"), None), P(("row", "col"), None)),
        check_vma=False,
    )
```

profile of v0, /device:TPU:0, one launch (start us, length us, event | category | flops | bytes accessed | tf_op | source)
XLA Modules:
  0.0 448.6 jit_solution(699449108784459341)
XLA Ops:
  7.2 0.7 compare_convert_fusion
  8.0 1.7 fusion.14
  9.7 7.4 %all-to-all-start = ((bf16[64,128,128]{2,1,0:T(8,128)(2,1)}), bf16[64,128,128]{2,1,0:T(8,128)(2,1)}, u32[]{:S(2)}, u32[]{:S(2)}) async-start(bf16[64,128,128]{2,1,0:T(8,128)(2,1)} %bitcast.112), calls=%async_computation.3 | async-start | bytes 4194304 | tf_op jit(solution)/shard_map/all_to_all | solution.py:74
  18.0 51.4 %all-gather.7.cloned.1.call-done = bf16[4096,128]{1,0:T(8,128)(2,1)} async-done(((bf16[512,128]{1,0:T(8,128)(2,1)}), bf16[4096,128]{1,0:T(8,128)(2,1)}) %all-gather.7.cloned.1.call-update) | async-done | bytes 1048592 | tf_op jit(solution)/shard_map/all_gather | solution.py:12
  69.4 3.6 gather_fusion
  73.0 5.1 %fusion.49 = f32[64,128,128]{2,1,0:T(8,128)} fusion(bf16[64,128,128]{2,1,0:T(8,128)(2,1)} %gather_fusion, bf16[1,1,64,128,128]{4,3,2,1,0:T(8,128)(2,1)S(1)} %copy-done), kind=kOutput, calls=%fused_computation.99 | convolution fusion | flops 268435456 | bytes 8388608 | tf_op jit(solution)/shard_map/ntk,nks->nts/dot_general | solution.py:14
  78.2 5.4 %copy.13 = f32[64,128,128]{1,0,2:T(8,128)} copy(f32[64,128,128]{2,1,0:T(8,128)} %fusion.49) | data formatting | bytes 8388608 | tf_op jit(solution)/shard_map/ntk,nks->nts/dot_general | solution.py:14
  83.5 3.7 fusion.10
  87.2 1.3 copy.7
  88.9 21.0 %all-gather.13.cloned.1.call-done = bf16[4096,128]{1,0:T(8,128)(2,1)} async-done(((bf16[512,128]{1,0:T(8,128)(2,1)}), bf16[4096,128]{1,0:T(8,128)(2,1)}) %all-gather.13.cloned.1.call-update) | async-done | bytes 1048592 | tf_op jit(solution)/shard_map/all_gather | solution.py:26
  109.9 3.4 gather_fusion.3
  113.3 5.1 %fusion.51 = f32[64,128,128]{2,1,0:T(8,128)} fusion(bf16[64,128,128]{2,1,0:T(8,128)(2,1)} %gather_fusion.3, bf16[64,128,128]{2,1,0:T(8,128)(2,1)} %all-to-all-done), kind=kOutput, calls=%fused_computation.101 | convolution fusion | flops 268435456 | bytes 8388608 | tf_op jit(solution)/shard_map/nkt,nks->nts/dot_general | solution.py:28
  118.4 5.5 %copy.16 = f32[64,128,128]{1,0,2:T(8,128)} copy(f32[64,128,128]{2,1,0:T(8,128)} %fusion.51) | data formatting | bytes 8388608 | tf_op jit(solution)/shard_map/nkt,nks->nts/dot_general | solution.py:28
  123.9 3.7 fusion.4
  127.5 1.3 copy.10
  128.9 7.2 %reduce-scatter.7.cloned.1.call-done = f32[512,128]{1,0:T(8,128)} async-done(((f32[2048,128]{1,0:T(8,128)}), f32[512,128]{1,0:T(8,128)}) %reduce-scatter.7.cloned.1.call-update) | async-done | bytes 262160 | tf_op jit(solution)/shard_map/reduce_scatter | solution.py:19
  136.1 27.5 %reduce-scatter.13.cloned.1.call-done = f32[512,128]{1,0:T(8,128)} async-done(((f32[2048,128]{1,0:T(8,128)}), f32[512,128]{1,0:T(8,128)}) %reduce-scatter.13.cloned.1.call-update) | async-done | bytes 262160 | tf_op jit(solution)/shard_map/reduce_scatter | solution.py:33
  163.6 1.8 fusion.18
  166.2 40.1 %all-gather.15.cloned.1.call-done = bf16[4096,128]{1,0:T(8,128)(2,1)} async-done(((bf16[512,128]{1,0:T(8,128)(2,1)}), bf16[4096,128]{1,0:T(8,128)(2,1)}) %all-gather.15.cloned.1.call-update) | async-done | bytes 1048592 | tf_op jit(solution)/shard_map/all_gather | solution.py:26
  206.3 3.4 gather_fusion.4
  209.7 5.1 %fusion.52 = f32[64,128,128]{2,1,0:T(8,128)} fusion(bf16[64,128,128]{2,1,0:T(8,128)(2,1)} %gather_fusion.4, bf16[64,128,128]{2,1,0:T(8,128)(2,1)} %all-to-all-done), kind=kOutput, calls=%fused_computation.102 | convolution fusion | flops 268435456 | bytes 8388608 | tf_op jit(solution)/shard_map/nkt,nks->nts/dot_general | solution.py:28
  214.8 5.4 %copy.17 = f32[64,128,128]{1,0,2:T(8,128)} copy(f32[64,128,128]{2,1,0:T(8,128)} %fusion.52) | data formatting | bytes 8388608 | tf_op jit(solution)/shard_map/nkt,nks->nts/dot_general | solution.py:28
  220.2 3.7 fusion.2
  223.9 1.3 copy.11
  225.3 22.5 %all-gather.9.cloned.1.call-done = bf16[4096,128]{1,0:T(8,128)(2,1)} async-done(((bf16[512,128]{1,0:T(8,128)(2,1)}), bf16[4096,128]{1,0:T(8,128)(2,1)}) %all-gather.9.cloned.1.call-update) | async-done | bytes 1048592 | tf_op jit(solution)/shard_map/all_gather | solution.py:12
  247.8 3.4 gather_fusion.1
  251.2 5.2 %fusion.47 = f32[64,128,128]{2,1,0:T(8,128)} fusion(bf16[64,128,128]{2,1,0:T(8,128)(2,1)} %gather_fusion.1, bf16[1,1,64,128,128]{4,3,2,1,0:T(8,128)(2,1)S(1)} %copy-done), kind=kOutput, calls=%fused_computation.97 | convolution fusion | flops 268435456 | bytes 8388608 | tf_op jit(solution)/shard_map/ntk,nks->nts/dot_general | solution.py:14
  256.4 5.5 %copy.14 = f32[64,128,128]{1,0,2:T(8,128)} copy(f32[64,128,128]{2,1,0:T(8,128)} %fusion.47) | data formatting | bytes 8388608 | tf_op jit(solution)/shard_map/ntk,nks->nts/dot_general | solution.py:14
  261.9 3.7 fusion.8
  265.5 1.3 copy.8
  266.9 7.1 %reduce-scatter.15.cloned.1.call-done = f32[512,128]{1,0:T(8,128)} async-done(((f32[2048,128]{1,0:T(8,128)}), f32[512,128]{1,0:T(8,128)}) %reduce-scatter.15.cloned.1.call-update) | async-done | bytes 262160 | tf_op jit(solution)/shard_map/reduce_scatter | solution.py:33
  274.1 27.6 %reduce-scatter.9.cloned.1.call-done = f32[512,128]{1,0:T(8,128)} async-done(((f32[2048,128]{1,0:T(8,128)}), f32[512,128]{1,0:T(8,128)}) %reduce-scatter.9.cloned.1.call-update) | async-done | bytes 262160 | tf_op jit(solution)/shard_map/reduce_scatter | solution.py:19
  301.7 1.8 fusion.19
  304.1 40.5 %all-gather.17.cloned.1.call-done = bf16[4096,128]{1,0:T(8,128)(2,1)} async-done(((bf16[512,128]{1,0:T(8,128)(2,1)}), bf16[4096,128]{1,0:T(8,128)(2,1)}) %all-gather.17.cloned.1.call-update) | async-done | bytes 1048592 | tf_op jit(solution)/shard_map/all_gather | solution.py:26
  344.6 3.4 gather_fusion.5
  348.0 5.1 %fusion.53 = f32[64,128,128]{2,1,0:T(8,128)} fusion(bf16[64,128,128]{2,1,0:T(8,128)(2,1)} %gather_fusion.5, bf16[64,128,128]{2,1,0:T(8,128)(2,1)} %all-to-all-done), kind=kOutput, calls=%fused_computation.103 | convolution fusion | flops 268435456 | bytes 8388608 | tf_op jit(solution)/shard_map/nkt,nks->nts/dot_general | solution.py:28
  353.1 5.4 %copy.18 = f32[64,128,128]{1,0,2:T(8,128)} copy(f32[64,128,128]{2,1,0:T(8,128)} %fusion.53) | data formatting | bytes 8388608 | tf_op jit(solution)/shard_map/nkt,nks->nts/dot_general | solution.py:28
  358.5 3.7 fusion
  362.2 1.4 copy.12
  363.8 22.2 %all-gather.11.cloned.1.call-done = bf16[4096,128]{1,0:T(8,128)(2,1)} async-done(((bf16[512,128]{1,0:T(8,128)(2,1)}), bf16[4096,128]{1,0:T(8,128)(2,1)}) %all-gather.11.cloned.1.call-update) | async-done | bytes 1048592 | tf_op jit(solution)/shard_map/all_gather | solution.py:12
  386.1 3.4 gather_fusion.2
  389.5 5.2 %fusion.45 = f32[64,128,128]{2,1,0:T(8,128)} fusion(bf16[64,128,128]{2,1,0:T(8,128)(2,1)} %gather_fusion.2, bf16[1,1,64,128,128]{4,3,2,1,0:T(8,128)(2,1)S(1)} %copy-done), kind=kOutput, calls=%fused_computation.95 | convolution fusion | flops 268435456 | bytes 8388608 | tf_op jit(solution)/shard_map/ntk,nks->nts/dot_general | solution.py:14
  394.7 5.4 %copy.15 = f32[64,128,128]{1,0,2:T(8,128)} copy(f32[64,128,128]{2,1,0:T(8,128)} %fusion.45) | data formatting | bytes 8388608 | tf_op jit(solution)/shard_map/ntk,nks->nts/dot_general | solution.py:14
  400.1 3.6 fusion.6
  403.8 1.3 copy.9
  405.1 7.1 %reduce-scatter.17.cloned.1.call-done = f32[512,128]{1,0:T(8,128)} async-done(((f32[2048,128]{1,0:T(8,128)}), f32[512,128]{1,0:T(8,128)}) %reduce-scatter.17.cloned.1.call-update) | async-done | bytes 262160 | tf_op jit(solution)/shard_map/reduce_scatter | solution.py:33
  412.2 27.5 %reduce-scatter.11.cloned.1.call-done = f32[512,128]{1,0:T(8,128)} async-done(((f32[2048,128]{1,0:T(8,128)}), f32[512,128]{1,0:T(8,128)}) %reduce-scatter.11.cloned.1.call-update) | async-done | bytes 262160 | tf_op jit(solution)/shard_map/reduce_scatter | solution.py:19
  439.8 2.0 fusion.13
  (51 shorter events, 3.2 us)
Async XLA Ops:
  7.2 62.3 %all-gather.7.cloned.1.call-start = ((), (), s32[]{:S(2)}) async-start(), calls=%async_computation.7 | async-start | bytes 1179648 | tf_op jit(solution)/shard_map/all_gather | solution.py:12
  9.7 8.3 %copy-start.7 = (s32[8,4,64]{2,1,0:T(4,128)S(1)}, s32[8,4,64]{2,1,0:T(4,128)}, u32[]{:S(2)}) copy-start(s32[8,4,64]{2,1,0:T(4,128)} %param.6) | copy-start | bytes 24580
  9.7 103.6 %all-to-all-start = ((bf16[64,128,128]{2,1,0:T(8,128)(2,1)}), bf16[64,128,128]{2,1,0:T(8,128)(2,1)}, u32[]{:S(2)}, u32[]{:S(2)}) async-start(bf16[64,128,128]{2,1,0:T(8,128)(2,1)} %bitcast.112), calls=%async_computation.3 | async-start | bytes 4194304 | tf_op jit(solution)/shard_map/all_to_all | solution.py:74
  17.2 92.8 %all-gather.13.cloned.1.call-start = ((), (), s32[]{:S(2)}) async-start(), calls=%async_computation.13 | async-start | bytes 1179648 | tf_op jit(solution)/shard_map/all_gather | solution.py:26
  17.9 118.2 %reduce-scatter.7.cloned.1.call-start = ((), (), s32[]{:S(2)}) async-start(), calls=%async_computation.8 | async-start | bytes 1310720 | tf_op jit(solution)/shard_map/reduce_scatter | solution.py:19
  69.4 3.6 copy-start
  88.5 75.1 %reduce-scatter.13.cloned.1.call-start = ((), (), s32[]{:S(2)}) async-start(), calls=%async_computation.14 | async-start | bytes 1310720 | tf_op jit(solution)/shard_map/reduce_scatter | solution.py:33
  128.9 77.5 %all-gather.15.cloned.1.call-start = ((), (), s32[]{:S(2)}) async-start(), calls=%async_computation.15 | async-start | bytes 1179648 | tf_op jit(solution)/shard_map/all_gather | solution.py:26
  165.4 82.4 %all-gather.9.cloned.1.call-start = ((), (), s32[]{:S(2)}) async-start(), calls=%async_computation.9 | async-start | bytes 1179648 | tf_op jit(solution)/shard_map/all_gather | solution.py:12
  166.0 108.1 %reduce-scatter.15.cloned.1.call-start = ((), (), s32[]{:S(2)}) async-start(), calls=%async_computation.16 | async-start | bytes 1310720 | tf_op jit(solution)/shard_map/reduce_scatter | solution.py:33
  225.3 76.4 %reduce-scatter.9.cloned.1.call-start = ((), (), s32[]{:S(2)}) async-start(), calls=%async_computation.10 | async-start | bytes 1310720 | tf_op jit(solution)/shard_map/reduce_scatter | solution.py:19
  266.9 77.7 %all-gather.17.cloned.1.call-start = ((), (), s32[]{:S(2)}) async-start(), calls=%async_computation.17 | async-start | bytes 1179648 | tf_op jit(solution)/shard_map/all_gather | solution.py:26
  303.5 82.6 %all-gather.11.cloned.1.call-start = ((), (), s32[]{:S(2)}) async-start(), calls=%async_computation.11 | async-start | bytes 1179648 | tf_op jit(solution)/shard_map/all_gather | solution.py:12
  304.1 108.2 %reduce-scatter.17.cloned.1.call-start = ((), (), s32[]{:S(2)}) async-start(), calls=%async_computation.18 | async-start | bytes 1310720 | tf_op jit(solution)/shard_map/reduce_scatter | solution.py:33
  363.6 76.2 %reduce-scatter.11.cloned.1.call-start = ((), (), s32[]{:S(2)}) async-start(), calls=%async_computation.12 | async-start | bytes 1310720 | tf_op jit(solution)/shard_map/reduce_scatter | solution.py:19
  403.7 36.0 %copy-start.1 = (f32[512,128]{1,0:T(8,128)S(1)}, f32[512,128]{1,0:T(8,128)}, u32[]{:S(2)}) copy-start(f32[512,128]{1,0:T(8,128)} %reduce-scatter.7.cloned.1.call-done) | copy-start | bytes 786436
  403.8 36.0 %copy-start.2 = (f32[512,128]{1,0:T(8,128)S(1)}, f32[512,128]{1,0:T(8,128)}, u32[]{:S(2)}) copy-start(f32[512,128]{1,0:T(8,128)} %reduce-scatter.13.cloned.1.call-done) | copy-start | bytes 786436
  403.8 36.0 %copy-start.3 = (f32[512,128]{1,0:T(8,128)S(1)}, f32[512,128]{1,0:T(8,128)}, u32[]{:S(2)}) copy-start(f32[512,128]{1,0:T(8,128)} %reduce-scatter.15.cloned.1.call-done) | copy-start | bytes 786436
  403.8 36.0 %copy-start.4 = (f32[512,128]{1,0:T(8,128)S(1)}, f32[512,128]{1,0:T(8,128)}, u32[]{:S(2)}) copy-start(f32[512,128]{1,0:T(8,128)} %reduce-scatter.9.cloned.1.call-done) | copy-start | bytes 786436
  403.8 36.0 %copy-start.5 = (bf16[512,128]{1,0:T(8,128)(2,1)S(1)}, bf16[512,128]{1,0:T(8,128)(2,1)}, u32[]{:S(2)}) copy-start(bf16[512,128]{1,0:T(8,128)(2,1)} %param.8) | copy-start | bytes 393220
  403.8 36.0 %copy-start.6 = (bf16[512,128]{1,0:T(8,128)(2,1)S(1)}, bf16[512,128]{1,0:T(8,128)(2,1)}, u32[]{:S(2)}) copy-start(bf16[512,128]{1,0:T(8,128)(2,1)} %param.7) | copy-start | bytes 393220
Sparse Core Ops, SparseCore 0:
  10.7 58.6 all-gather.6
  72.1 37.7 all-gather.12
  112.5 23.6 reduce-scatter.6
  138.7 24.8 reduce-scatter.12
  166.2 40.1 all-gather.14
  208.9 38.8 all-gather.8
  250.4 23.6 reduce-scatter.14
  276.7 24.8 reduce-scatter.8
  304.4 40.1 all-gather.16
  347.1 38.8 all-gather.10
  388.6 23.6 reduce-scatter.16
  414.8 24.8 reduce-scatter.10
where the time goes:
time: 450 us; the launch traced here: 449 us
  waiting for transfers between devices  304 us (68%)
  local copies, waits for them, and re-layouts  61.3 us (14%)
  matrix products  52.8 us (12%)
  between operations  14.4 us (3%)
  starting transfers between devices  8.32 us (2%)
  other arithmetic  8.04 us (2%)
    all_gather x3, waiting for transfers between devices, charge_term(): gathered = lax.all_gather(vector, 'row', axis=0, tiled=True)  102 us
    all_gather x3, waiting for transfers between devices, supply_term(): gathered = lax.all_gather(vector, 'row', axis=0, tiled=True)  96.2 us
    reduce_scatter x3, waiting for transfers between devices, supply_term(): lax.psum_scatter(partial_value.reshape(-1, scenarios), 'col', scatter_dim...  62.3 us
    reduce_scatter x3, waiting for transfers between devices, charge_term(): lax.psum_scatter(partial_value.reshape(-1, scenarios), 'col', scatter_dim...  41.7 us
    dot_general x3, local copies, waits for them, and re-layouts, charge_term(): jnp.einsum('nkt,nks->nts', moved_tiles, picked, preferred_element_type=jn...  16.3 us
    dot_general x3, local copies, waits for them, and re-layouts, supply_term(): jnp.einsum('ntk,nks->nts', own_tiles, picked, preferred_element_type=jnp....  16.3 us
    dot_general x3, matrix products, supply_term(): jnp.einsum('ntk,nks->nts', own_tiles, picked, preferred_element_type=jnp....  15.5 us
    dot_general x3, matrix products, charge_term(): jnp.einsum('nkt,nks->nts', moved_tiles, picked, preferred_element_type=jn...  15.3 us
  transfers between devices with their start and end apart: 13, of which 12 were waited for; matrix products, arithmetic and copies ran while one was open for 25% of the time, Pallas kernels for 0%

commit v1 on v0

--- a/solution.py
+++ b/solution.py
@@ -9,7 +9,15 @@
 
 def supply_term(vector, own_tiles, local_rows, local_columns, block_rows, tile_size):
     scenarios = vector.shape[1]
-    gathered = lax.all_gather(vector, "row", axis=0, tiled=True)
+    ways, here = (lax.axis_size("row"), lax.axis_index("row"))
+    grown, reach = (vector, 1)
+    while reach < ways:
+        theirs = lax.ppermute(grown, "row", [(d, d ^ reach) for d in range(ways)])
+        mine_first = jnp.concatenate([grown, theirs], axis=0)
+        theirs_first = jnp.concatenate([theirs, grown], axis=0)
+        grown = jnp.where(here & reach == 0, mine_first, theirs_first)
+        reach = 2 * reach
+    gathered = grown
     picked = gathered.reshape(-1, tile_size, scenarios)[local_columns]
     products = jnp.einsum("ntk,nks->nts", own_tiles, picked, preferred_element_type=jnp.float32)
     selector = (jnp.arange(block_rows, dtype=jnp.int32)[:, None] == local_rows[None, :]).astype(

time: 450 us -> 405 us (0.900)
  waiting for transfers between devices: 304 us -> 246 us
  starting transfers between devices: 8.32 us -> 25.6 us
  local copies, waits for them, and re-layouts: 61.3 us -> 56.2 us
    ppermute x0 -> x9, waiting for transfers between devices: none -> 146 us  [supply_term(): theirs = lax.ppermute(grown, 'row', [(d, d ^ reach) for d in range(ways)])]
    all_gather x3 -> x0, waiting for transfers between devices: 96.2 us -> none  [supply_term(): gathered = lax.all_gather(vector, 'row', axis=0, tiled=True)]
    all_gather x3, waiting for transfers between devices: 102 us -> 5.97 us  [charge_term(): gathered = lax.all_gather(vector, 'row', axis=0, tiled=True)]
    reduce_scatter x3, waiting for transfers between devices: 62.3 us -> 12.2 us  [supply_term(): lax.psum_scatter(partial_value.reshape(-1, scenarios), 'col', scatter_dim...]
    reduce_scatter x3, waiting for transfers between devices: 41.7 us -> 82.5 us  [charge_term(): lax.psum_scatter(partial_value.reshape(-1, scenarios), 'col', scatter_dim...]
    ppermute x0 -> x9, starting transfers between devices: none -> 17.3 us  [supply_term(): theirs = lax.ppermute(grown, 'row', [(d, d ^ reach) for d in range(ways)])]
  transfers between devices with their start and end apart: 13 -> 19, of which waited for: 12 -> 17; matrix products, arithmetic and copies ran while one was open for 25% -> 27% of each run, Pallas kernels for 0% -> 0%
where the time goes in v1:
time: 405 us; the launch traced here: 404 us
  waiting for transfers between devices  246 us (61%)
  local copies, waits for them, and re-layouts  56.2 us (14%)
  matrix products  52.8 us (13%)
  starting transfers between devices  25.6 us (6%)
  between operations  15.5 us (4%)
  other arithmetic  7.77 us (2%)
    ppermute x9, waiting for transfers between devices, supply_term(): theirs = lax.ppermute(grown, 'row', [(d, d ^ reach) for d in range(ways)])  146 us
    reduce_scatter x3, waiting for transfers between devices, charge_term(): lax.psum_scatter(partial_value.reshape(-1, scenarios), 'col', scatter_dim...  82.5 us
    ppermute x9, starting transfers between devices, supply_term(): theirs = lax.ppermute(grown, 'row', [(d, d ^ reach) for d in range(ways)])  17.3 us
    dot_general x3, local copies, waits for them, and re-layouts, supply_term(): jnp.einsum('ntk,nks->nts', own_tiles, picked, preferred_element_type=jnp....  16.2 us
    dot_general x3, local copies, waits for them, and re-layouts, charge_term(): jnp.einsum('nkt,nks->nts', moved_tiles, picked, preferred_element_type=jn...  16.2 us
    dot_general x3, matrix products, supply_term(): jnp.einsum('ntk,nks->nts', own_tiles, picked, preferred_element_type=jnp....  15.5 us
    dot_general x3, matrix products, charge_term(): jnp.einsum('nkt,nks->nts', moved_tiles, picked, preferred_element_type=jn...  14.9 us
    reduce_scatter x3, waiting for transfers between devices, supply_term(): lax.psum_scatter(partial_value.reshape(-1, scenarios), 'col', scatter_dim...  12.2 us
  transfers between devices with their start and end apart: 19, of which 17 were waited for; matrix products, arithmetic and copies ran while one was open for 27% of the time, Pallas kernels for 0%

profile of v1, /device:TPU:0, one launch (start us, length us, event | category | flops | bytes accessed | tf_op | source)
XLA Modules:
  0.0 404.3 jit_solution(9604293863486950648)
XLA Ops:
  8.0 7.4 %all-to-all-start = ((bf16[64,128,128]{2,1,0:T(8,128)(2,1)}), bf16[64,128,128]{2,1,0:T(8,128)(2,1)}, u32[]{:S(2)}, u32[]{:S(2)}) async-start(bf16[64,128,128]{2,1,0:T(8,128)(2,1)} %bitcast.112), calls=%async_computation.3 | async-start | bytes 4194304 | tf_op jit(solution)/shard_map/all_to_all | solution.py:82
  18.0 18.0 %collective-permute-done = bf16[512,128]{1,0:T(8,128)(2,1)S(1)} collective-permute-done((bf16[512,128]{1,0:T(8,128)(2,1)S(1)}, bf16[512,128]{1,0:T(8,128)(2,1)S(1)}, u32[]{:S(2)}, u32[]{:S(2)}) %collective-permute-start) | collective-permute-done | bytes 131104 | tf_op jit(solution)/shard_map/ppermute | solution.py:15
  36.3 23.5 %collective-permute-done.1 = bf16[1024,128]{1,0:T(8,128)(2,1)S(1)} collective-permute-done((bf16[1024,128]{1,0:T(8,128)(2,1)S(1)}, bf16[1024,128]{1,0:T(8,128)(2,1)S(1)}, u32[]{:S(2)}, u32[]{:S(2)}) %collective-permute-start.1) | collective-permute-done | bytes 262176 | tf_op jit(solution)/shard_map/ppermute | solution.py:15
  59.9 4.6 %collective-permute-start.2 = (bf16[2048,128]{1,0:T(8,128)(2,1)S(1)}, bf16[2048,128]{1,0:T(8,128)(2,1)S(1)}, u32[]{:S(2)}, u32[]{:S(2)}) collective-permute-start(bf16[2048,128]{1,0:T(8,128)(2,1)S(1)} %maximum_select_fusion.3), channel_id=1, source_target_pairs={{0,16},{4,20},{8,24},{12,28},{16,0},{20,4},{24,8},{28,12},{1,17},{... | collective-permute-start | bytes 1572872 | tf_op jit(solution)/shard_map/ppermute | solution.py:15
  64.6 34.7 %collective-permute-done.2 = bf16[2048,128]{1,0:T(8,128)(2,1)S(1)} collective-permute-done((bf16[2048,128]{1,0:T(8,128)(2,1)S(1)}, bf16[2048,128]{1,0:T(8,128)(2,1)S(1)}, u32[]{:S(2)}, u32[]{:S(2)}) %collective-permute-start.2) | collective-permute-done | bytes 524320 | tf_op jit(solution)/shard_map/ppermute | solution.py:15
  99.6 2.2 gather_fusion
  101.8 5.2 %fusion.49 = f32[64,128,128]{2,1,0:T(8,128)} fusion(bf16[64,128,128]{2,1,0:T(8,128)(2,1)} %gather_fusion, bf16[1,1,64,128,128]{4,3,2,1,0:T(8,128)(2,1)S(1)} %copy-done), kind=kOutput, calls=%fused_computation.108 | convolution fusion | flops 268435456 | bytes 8388608 | tf_op jit(solution)/shard_map/ntk,nks->nts/dot_general | solution.py:22
  106.9 5.4 %copy.13 = f32[64,128,128]{1,0,2:T(8,128)} copy(f32[64,128,128]{2,1,0:T(8,128)} %fusion.49) | data formatting | bytes 8388608 | tf_op jit(solution)/shard_map/ntk,nks->nts/dot_general | solution.py:22
  112.3 3.7 fusion.10
  117.7 3.4 gather_fusion.3
  121.2 5.2 %fusion.51 = f32[64,128,128]{2,1,0:T(8,128)} fusion(bf16[64,128,128]{2,1,0:T(8,128)(2,1)} %gather_fusion.3, bf16[64,128,128]{2,1,0:T(8,128)(2,1)} %all-to-all-done), kind=kOutput, calls=%fused_computation.110 | convolution fusion | flops 268435456 | bytes 8388608 | tf_op jit(solution)/shard_map/nkt,nks->nts/dot_general | solution.py:36
  126.4 5.4 %copy.16 = f32[64,128,128]{1,0,2:T(8,128)} copy(f32[64,128,128]{2,1,0:T(8,128)} %fusion.51) | data formatting | bytes 8388608 | tf_op jit(solution)/shard_map/nkt,nks->nts/dot_general | solution.py:36
  131.8 3.8 fusion.4
  137.0 4.8 %reduce-scatter.7.cloned.1.call-done = f32[512,128]{1,0:T(8,128)} async-done(((f32[2048,128]{1,0:T(8,128)}), f32[512,128]{1,0:T(8,128)}) %reduce-scatter.7.cloned.1.call-update) | async-done | bytes 262160 | tf_op jit(solution)/shard_map/reduce_scatter | solution.py:27
  141.8 27.4 %reduce-scatter.13.cloned.1.call-done = f32[512,128]{1,0:T(8,128)} async-done(((f32[2048,128]{1,0:T(8,128)}), f32[512,128]{1,0:T(8,128)}) %reduce-scatter.13.cloned.1.call-update) | async-done | bytes 262160 | tf_op jit(solution)/shard_map/reduce_scatter | solution.py:41
  169.2 1.7 fusion.18
  172.4 3.7 collective-permute-done.3
  177.9 5.3 %collective-permute-done.4 = bf16[1024,128]{1,0:T(8,128)(2,1)S(1)} collective-permute-done((bf16[1024,128]{1,0:T(8,128)(2,1)S(1)}, bf16[1024,128]{1,0:T(8,128)(2,1)S(1)}, u32[]{:S(2)}, u32[]{:S(2)}) %collective-permute-start.4) | collective-permute-done | bytes 262176 | tf_op jit(solution)/shard_map/ppermute | solution.py:15
  183.4 2.5 collective-permute-start.5
  185.8 25.8 %collective-permute-done.5 = bf16[2048,128]{1,0:T(8,128)(2,1)S(1)} collective-permute-done((bf16[2048,128]{1,0:T(8,128)(2,1)S(1)}, bf16[2048,128]{1,0:T(8,128)(2,1)S(1)}, u32[]{:S(2)}, u32[]{:S(2)}) %collective-permute-start.5) | collective-permute-done | bytes 524320 | tf_op jit(solution)/shard_map/ppermute | solution.py:15
  211.9 2.2 gather_fusion.1
  214.1 5.2 %fusion.47 = f32[64,128,128]{2,1,0:T(8,128)} fusion(bf16[64,128,128]{2,1,0:T(8,128)(2,1)} %gather_fusion.1, bf16[1,1,64,128,128]{4,3,2,1,0:T(8,128)(2,1)S(1)} %copy-done), kind=kOutput, calls=%fused_computation.106 | convolution fusion | flops 268435456 | bytes 8388608 | tf_op jit(solution)/shard_map/ntk,nks->nts/dot_general | solution.py:22
  219.3 5.4 %copy.14 = f32[64,128,128]{1,0,2:T(8,128)} copy(f32[64,128,128]{2,1,0:T(8,128)} %fusion.47) | data formatting | bytes 8388608 | tf_op jit(solution)/shard_map/ntk,nks->nts/dot_general | solution.py:22
  224.7 3.7 fusion.8
  229.7 3.0 all-gather.6.cloned.1.call-done
  232.7 3.4 gather_fusion.4
  236.2 5.3 %fusion.52 = f32[64,128,128]{2,1,0:T(8,128)} fusion(bf16[64,128,128]{2,1,0:T(8,128)(2,1)} %gather_fusion.4, bf16[64,128,128]{2,1,0:T(8,128)(2,1)} %all-to-all-done), kind=kOutput, calls=%fused_computation.111 | convolution fusion | flops 268435456 | bytes 8388608 | tf_op jit(solution)/shard_map/nkt,nks->nts/dot_general | solution.py:36
  241.4 5.4 %copy.17 = f32[64,128,128]{1,0,2:T(8,128)} copy(f32[64,128,128]{2,1,0:T(8,128)} %fusion.52) | data formatting | bytes 8388608 | tf_op jit(solution)/shard_map/nkt,nks->nts/dot_general | solution.py:36
  246.8 3.7 fusion.2
  251.9 2.7 reduce-scatter.9.cloned.1.call-done
  254.6 27.6 %reduce-scatter.15.cloned.1.call-done = f32[512,128]{1,0:T(8,128)} async-done(((f32[2048,128]{1,0:T(8,128)}), f32[512,128]{1,0:T(8,128)}) %reduce-scatter.15.cloned.1.call-update) | async-done | bytes 262160 | tf_op jit(solution)/shard_map/reduce_scatter | solution.py:41
  282.1 1.7 fusion.19
  285.4 3.7 collective-permute-done.6
  291.0 5.3 %collective-permute-done.7 = bf16[1024,128]{1,0:T(8,128)(2,1)S(1)} collective-permute-done((bf16[1024,128]{1,0:T(8,128)(2,1)S(1)}, bf16[1024,128]{1,0:T(8,128)(2,1)S(1)}, u32[]{:S(2)}, u32[]{:S(2)}) %collective-permute-start.7) | collective-permute-done | bytes 262176 | tf_op jit(solution)/shard_map/ppermute | solution.py:15
  296.4 2.4 collective-permute-start.8
  298.8 25.9 %collective-permute-done.8 = bf16[2048,128]{1,0:T(8,128)(2,1)S(1)} collective-permute-done((bf16[2048,128]{1,0:T(8,128)(2,1)S(1)}, bf16[2048,128]{1,0:T(8,128)(2,1)S(1)}, u32[]{:S(2)}, u32[]{:S(2)}) %collective-permute-start.8) | collective-permute-done | bytes 524320 | tf_op jit(solution)/shard_map/ppermute | solution.py:15
  325.0 2.2 gather_fusion.2
  327.2 5.2 %fusion.45 = f32[64,128,128]{2,1,0:T(8,128)} fusion(bf16[64,128,128]{2,1,0:T(8,128)(2,1)} %gather_fusion.2, bf16[1,1,64,128,128]{4,3,2,1,0:T(8,128)(2,1)S(1)} %copy-done), kind=kOutput, calls=%fused_computation.104 | convolution fusion | flops 268435456 | bytes 8388608 | tf_op jit(solution)/shard_map/ntk,nks->nts/dot_general | solution.py:22
  332.3 5.4 %copy.15 = f32[64,128,128]{1,0,2:T(8,128)} copy(f32[64,128,128]{2,1,0:T(8,128)} %fusion.45) | data formatting | bytes 8388608 | tf_op jit(solution)/shard_map/ntk,nks->nts/dot_general | solution.py:22
  337.7 3.7 fusion.6
  342.8 2.9 all-gather.8.cloned.1.call-done
  345.7 2.2 gather_fusion.5
  347.9 4.4 %fusion.53 = f32[64,128,128]{2,1,0:T(8,128)} fusion(bf16[64,128,128]{2,1,0:T(8,128)(2,1)S(1)} %gather_fusion.5, bf16[64,128,128]{2,1,0:T(8,128)(2,1)} %all-to-all-done), kind=kOutput, calls=%fused_computation.112 | convolution fusion | flops 268435456 | bytes 8388608 | tf_op jit(solution)/shard_map/nkt,nks->nts/dot_general | solution.py:36
  352.3 5.4 %copy.18 = f32[64,128,128]{1,0,2:T(8,128)} copy(f32[64,128,128]{2,1,0:T(8,128)} %fusion.53) | data formatting | bytes 8388608 | tf_op jit(solution)/shard_map/nkt,nks->nts/dot_general | solution.py:36
  357.8 3.8 fusion
  363.0 4.7 %reduce-scatter.11.cloned.1.call-done = f32[512,128]{1,0:T(8,128)} async-done(((f32[2048,128]{1,0:T(8,128)}), f32[512,128]{1,0:T(8,128)}) %reduce-scatter.11.cloned.1.call-update) | async-done | bytes 262160 | tf_op jit(solution)/shard_map/reduce_scatter | solution.py:27
  367.6 27.5 %reduce-scatter.17.cloned.1.call-done = f32[512,128]{1,0:T(8,128)} async-done(((f32[2048,128]{1,0:T(8,128)}), f32[512,128]{1,0:T(8,128)}) %reduce-scatter.17.cloned.1.call-update) | async-done | bytes 262160 | tf_op jit(solution)/shard_map/reduce_scatter | solution.py:41
  395.2 2.0 fusion.13
  (71 shorter events, 19.3 us)
Async XLA Ops:
  8.0 7.6 %copy-start.8 = (s32[128]{0:T(128)S(1)}, s32[128]{0:T(128)}, u32[]{:S(2)}) copy-start(s32[128]{0:T(128)} %param.9) | copy-start | bytes 1540
  8.0 7.6 %copy-start.5 = (bf16[512,128]{1,0:T(8,128)(2,1)S(1)}, bf16[512,128]{1,0:T(8,128)(2,1)}, u32[]{:S(2)}) copy-start(bf16[512,128]{1,0:T(8,128)(2,1)} %param.8) | copy-start | bytes 393220
  8.0 7.6 %copy-start.6 = (bf16[512,128]{1,0:T(8,128)(2,1)S(1)}, bf16[512,128]{1,0:T(8,128)(2,1)}, u32[]{:S(2)}) copy-start(bf16[512,128]{1,0:T(8,128)(2,1)} %param.7) | copy-start | bytes 393220
  8.0 113.1 %all-to-all-start = ((bf16[64,128,128]{2,1,0:T(8,128)(2,1)}), bf16[64,128,128]{2,1,0:T(8,128)(2,1)}, u32[]{:S(2)}, u32[]{:S(2)}) async-start(bf16[64,128,128]{2,1,0:T(8,128)(2,1)} %bitcast.112), calls=%async_computation.3 | async-start | bytes 4194304 | tf_op jit(solution)/shard_map/all_to_all | solution.py:82
  15.5 49.1 %copy-start.7 = (s32[8,4,64]{2,1,0:T(4,128)S(1)}, s32[8,4,64]{2,1,0:T(4,128)}, u32[]{:S(2)}) copy-start(s32[8,4,64]{2,1,0:T(4,128)} %param.6) | copy-start | bytes 24580
  15.5 102.3 %all-gather.4.cloned.1.call-start = ((), (), s32[]{:S(2)}) async-start(), calls=%async_computation.10 | async-start | bytes 1179648 | tf_op jit(solution)/shard_map/all_gather | solution.py:34
  16.3 19.7 %collective-permute-start = (bf16[512,128]{1,0:T(8,128)(2,1)S(1)}, bf16[512,128]{1,0:T(8,128)(2,1)S(1)}, u32[]{:S(2)}, u32[]{:S(2)}) collective-permute-start(bf16[512,128]{1,0:T(8,128)(2,1)S(1)} %get-tuple-element.9), channel_id=1, source_target_pairs={{0,4},{4,0},{8,12},{12,8},{16,20},{20,16},{24,28},{28,24},{1,5},{5... | collective-permute-start | bytes 393224 | tf_op jit(solution)/shard_map/ppermute | solution.py:15
  36.1 23.7 %collective-permute-start.1 = (bf16[1024,128]{1,0:T(8,128)(2,1)S(1)}, bf16[1024,128]{1,0:T(8,128)(2,1)S(1)}, u32[]{:S(2)}, u32[]{:S(2)}) collective-permute-start(bf16[1024,128]{1,0:T(8,128)(2,1)S(1)} %maximum_select_fusion.6), channel_id=1, source_target_pairs={{0,8},{4,12},{8,0},{12,4},{16,24},{20,28},{24,16},{28,20},{1,9},{5... | collective-permute-start | bytes 786440 | tf_op jit(solution)/shard_map/ppermute | solution.py:15
  36.2 105.6 %reduce-scatter.7.cloned.1.call-start = ((), (), s32[]{:S(2)}) async-start(), calls=%async_computation.7 | async-start | bytes 1310720 | tf_op jit(solution)/shard_map/reduce_scatter | solution.py:27
  59.9 39.4 %collective-permute-start.2 = (bf16[2048,128]{1,0:T(8,128)(2,1)S(1)}, bf16[2048,128]{1,0:T(8,128)(2,1)S(1)}, u32[]{:S(2)}, u32[]{:S(2)}) collective-permute-start(bf16[2048,128]{1,0:T(8,128)(2,1)S(1)} %maximum_select_fusion.3), channel_id=1, source_target_pairs={{0,16},{4,20},{8,24},{12,28},{16,0},{20,4},{24,8},{28,12},{1,17},{... | collective-permute-start | bytes 1572872 | tf_op jit(solution)/shard_map/ppermute | solution.py:15
  99.5 2.2 copy-start
  117.3 51.9 %reduce-scatter.13.cloned.1.call-start = ((), (), s32[]{:S(2)}) async-start(), calls=%async_computation.11 | async-start | bytes 1310720 | tf_op jit(solution)/shard_map/reduce_scatter | solution.py:41
  137.0 95.8 %all-gather.6.cloned.1.call-start = ((), (), s32[]{:S(2)}) async-start(), calls=%async_computation.12 | async-start | bytes 1179648 | tf_op jit(solution)/shard_map/all_gather | solution.py:34
  170.9 5.1 %collective-permute-start.3 = (bf16[512,128]{1,0:T(8,128)(2,1)S(1)}, bf16[512,128]{1,0:T(8,128)(2,1)S(1)}, u32[]{:S(2)}, u32[]{:S(2)}) collective-permute-start(bf16[512,128]{1,0:T(8,128)(2,1)S(1)} %get-tuple-element.7), channel_id=1, source_target_pairs={{0,4},{4,0},{8,12},{12,8},{16,20},{20,16},{24,28},{28,24},{1,5},{5... | collective-permute-start | bytes 393224 | tf_op jit(solution)/shard_map/ppermute | solution.py:15
  176.1 7.1 %collective-permute-start.4 = (bf16[1024,128]{1,0:T(8,128)(2,1)S(1)}, bf16[1024,128]{1,0:T(8,128)(2,1)S(1)}, u32[]{:S(2)}, u32[]{:S(2)}) collective-permute-start(bf16[1024,128]{1,0:T(8,128)(2,1)S(1)} %maximum_select_fusion.7), channel_id=1, source_target_pairs={{0,8},{4,12},{8,0},{12,4},{16,24},{20,28},{24,16},{28,20},{1,9},{5... | collective-permute-start | bytes 786440 | tf_op jit(solution)/shard_map/ppermute | solution.py:15
  177.7 76.9 %reduce-scatter.9.cloned.1.call-start = ((), (), s32[]{:S(2)}) async-start(), calls=%async_computation.8 | async-start | bytes 1310720 | tf_op jit(solution)/shard_map/reduce_scatter | solution.py:27
  183.4 28.3 %collective-permute-start.5 = (bf16[2048,128]{1,0:T(8,128)(2,1)S(1)}, bf16[2048,128]{1,0:T(8,128)(2,1)S(1)}, u32[]{:S(2)}, u32[]{:S(2)}) collective-permute-start(bf16[2048,128]{1,0:T(8,128)(2,1)S(1)} %maximum_select_fusion.4), channel_id=1, source_target_pairs={{0,16},{4,20},{8,24},{12,28},{16,0},{20,4},{24,8},{28,12},{1,17},{... | collective-permute-start | bytes 1572872 | tf_op jit(solution)/shard_map/ppermute | solution.py:15
  229.7 52.5 %reduce-scatter.15.cloned.1.call-start = ((), (), s32[]{:S(2)}) async-start(), calls=%async_computation.13 | async-start | bytes 1310720 | tf_op jit(solution)/shard_map/reduce_scatter | solution.py:41
  251.8 93.9 %all-gather.8.cloned.1.call-start = ((), (), s32[]{:S(2)}) async-start(), calls=%async_computation.14 | async-start | bytes 1179648 | tf_op jit(solution)/shard_map/all_gather | solution.py:34
  283.9 5.2 %collective-permute-start.6 = (bf16[512,128]{1,0:T(8,128)(2,1)S(1)}, bf16[512,128]{1,0:T(8,128)(2,1)S(1)}, u32[]{:S(2)}, u32[]{:S(2)}) collective-permute-start(bf16[512,128]{1,0:T(8,128)(2,1)S(1)} %get-tuple-element.5), channel_id=1, source_target_pairs={{0,4},{4,0},{8,12},{12,8},{16,20},{20,16},{24,28},{28,24},{1,5},{5... | collective-permute-start | bytes 393224 | tf_op jit(solution)/shard_map/ppermute | solution.py:15
  289.1 7.1 %collective-permute-start.7 = (bf16[1024,128]{1,0:T(8,128)(2,1)S(1)}, bf16[1024,128]{1,0:T(8,128)(2,1)S(1)}, u32[]{:S(2)}, u32[]{:S(2)}) collective-permute-start(bf16[1024,128]{1,0:T(8,128)(2,1)S(1)} %maximum_select_fusion.8), channel_id=1, source_target_pairs={{0,8},{4,12},{8,0},{12,4},{16,24},{20,28},{24,16},{28,20},{1,9},{5... | collective-permute-start | bytes 786440 | tf_op jit(solution)/shard_map/ppermute | solution.py:15
  290.7 76.9 %reduce-scatter.11.cloned.1.call-start = ((), (), s32[]{:S(2)}) async-start(), calls=%async_computation.9 | async-start | bytes 1310720 | tf_op jit(solution)/shard_map/reduce_scatter | solution.py:27
  296.4 28.3 %collective-permute-start.8 = (bf16[2048,128]{1,0:T(8,128)(2,1)S(1)}, bf16[2048,128]{1,0:T(8,128)(2,1)S(1)}, u32[]{:S(2)}, u32[]{:S(2)}) collective-permute-start(bf16[2048,128]{1,0:T(8,128)(2,1)S(1)} %maximum_select_fusion.5), channel_id=1, source_target_pairs={{0,16},{4,20},{8,24},{12,28},{16,0},{20,4},{24,8},{28,12},{1,17},{... | collective-permute-start | bytes 1572872 | tf_op jit(solution)/shard_map/ppermute | solution.py:15
  342.7 52.4 %reduce-scatter.17.cloned.1.call-start = ((), (), s32[]{:S(2)}) async-start(), calls=%async_computation.15 | async-start | bytes 1310720 | tf_op jit(solution)/shard_map/reduce_scatter | solution.py:41
  361.6 33.6 %copy-start.1 = (f32[512,128]{1,0:T(8,128)S(1)}, f32[512,128]{1,0:T(8,128)}, u32[]{:S(2)}) copy-start(f32[512,128]{1,0:T(8,128)} %reduce-scatter.7.cloned.1.call-done) | copy-start | bytes 786436
  361.6 33.6 %copy-start.2 = (f32[512,128]{1,0:T(8,128)S(1)}, f32[512,128]{1,0:T(8,128)}, u32[]{:S(2)}) copy-start(f32[512,128]{1,0:T(8,128)} %reduce-scatter.13.cloned.1.call-done) | copy-start | bytes 786436
  361.6 33.6 %copy-start.3 = (f32[512,128]{1,0:T(8,128)S(1)}, f32[512,128]{1,0:T(8,128)}, u32[]{:S(2)}) copy-start(f32[512,128]{1,0:T(8,128)} %reduce-scatter.9.cloned.1.call-done) | copy-start | bytes 786436
  361.6 33.6 %copy-start.4 = (f32[512,128]{1,0:T(8,128)S(1)}, f32[512,128]{1,0:T(8,128)}, u32[]{:S(2)}) copy-start(f32[512,128]{1,0:T(8,128)} %reduce-scatter.15.cloned.1.call-done) | copy-start | bytes 786436
Sparse Core Ops, SparseCore 0:
  36.3 54.9 all-gather.3
  177.8 54.8 all-gather.5
  290.8 54.8 all-gather.7
Sparse Core Ops, SparseCore 1:
  117.4 24.3 reduce-scatter.6
  144.3 24.8 reduce-scatter.12
  229.8 24.8 reduce-scatter.8
  257.3 24.8 reduce-scatter.14
  342.8 24.7 reduce-scatter.10
  370.3 24.8 reduce-scatter.16
